TPU v7x, 512 devices: a whole 4x4x16 slice. The times are simulated.
512 devices in a mesh: row: 16 (over z), space: 32 (over y, x, core).
Axes of the slice: x: 4, y: 4, z: 16, core: 2. Of those that a mesh axis runs over, the one named last changes fastest.
Arguments:
- features: bfloat16 [8192, 128], P(('row', 'space')), may hold values from -6 to 6
- positions: float32 [3, 8192], P(None, ('row', 'space')), may hold values from -0.5 to 78, as said below
- species: int32 [8192], P(('row', 'space')), may hold values from 0 to 3
- ghost_list: int32 [16, 1024, 32], P('row', 'space'), may hold values from 0 to 15
- edge_recv: int32 [262144], P(('row', 'space')), may hold values from 0 to 16, as said below
- edge_send: int32 [262144], P(('row', 'space')), may hold values from 0 to 1039
- edge_vec: float32 [3, 262144], P(None, ('row', 'space')), may hold values from -5.8 to 5.8, as said below
- w_msg: bfloat16 [128, 256], replicated, may hold values from -0.5 to 0.5
- w_rad1: float32 [8, 128], replicated, may hold values from -2 to 2
- w_rad2: bfloat16 [128, 256], replicated, may hold values from -0.5 to 0.5
- w_up: bfloat16 [256, 128], replicated, may hold values from -0.375 to 0.375
- w_out: float32 [128], replicated, may hold values from -0.5 to 0.5
- hardness: float32 [4], replicated, may hold values from 2 to 4
- width: float32 [4], replicated, may hold values from 0.8 to 1.6
- chi_shift: float32 [4], replicated, may hold values from -1 to 1
- field: float32 [1], replicated, may hold values from 0.01 to 0.03
Outputs:
- new_features: bfloat16 [8192, 128], P(('row', 'space'))
- charges: float32 [8192], P(('row', 'space'))
- forces: float32 [3, 8192], P(None, ('row', 'space'))
- virial: float32 [6, 8192], P(None, ('row', 'space'))
Inputs may be any that keep to these rules, and one draw needn't show every extreme that they name: `edge_recv`: in every domain the edges are ordered by receiver; the slots in use fill the first whole blocks of 128 rows, a quarter of the blocks or more, and the other slots hold 16; some domain uses all its slots. `positions`: every two atoms are 1.5 or more apart. `edge_vec`: each edge's length lies between 1.2 and 5.8.
All inputs are finite; a program needn't handle non-finite values.
Results may differ from a plain program's by a relative error of at most 0.0045.
Values may be sent and summed in bfloat16 or wider, within the bound.
A program may use at most 64 MiB of HBM per device.

v0:
```python
import math

import jax
import jax.numpy as jnp
from jax import lax
from jax.sharding import PartitionSpec as P

ITERS = 2


cutoff = 6.0
message_scale = 0.125
two_over_root_pi = 2.0 / math.sqrt(math.pi)
inverse_root_pi = 1.0 / math.sqrt(math.pi)
pair_limit = 262144


def lookup(species, table):
    result = jnp.zeros(species.shape, jnp.float32)
    for kind in range(table.shape[0]):
        result = result + jnp.where(species == kind, table[kind], 0.0)
    return result


def pair_block(target, target_labels, source, source_labels, source_charge, forces):
    delta = target[:3, :, None] - source[:3, None, :]
    squared = jnp.sum(delta * delta, axis=0)
    same = target_labels[:, None] == source_labels[None, :]
    squared = jnp.where(same, 1.0, squared)
    inverse = lax.rsqrt(squared)
    radius = squared * inverse
    spread = target[3][:, None] * target[3][:, None] + source[3][None, :] * source[3][None, :]
    scale = lax.rsqrt(2.0 * spread)
    scaled = radius * scale
    smear = lax.erf(scaled)
    if forces:
        slope = (
            two_over_root_pi * scale * jnp.exp(-scaled * scaled) * inverse
            - smear * inverse * inverse
        )
        weight = jnp.where(same, 0.0, source_charge[None, :] * slope * inverse)
        first = jnp.sum(weight[None] * delta, axis=2)
        pairs = ((0, 0), (1, 1), (2, 2), (0, 1), (0, 2), (1, 2))
        second = jnp.stack(
            [jnp.sum(weight * delta[left] * delta[right], axis=1) for left, right in pairs]
        )
        return jnp.concatenate([first, second], axis=0)
    kernel = jnp.where(same, 0.0, smear * inverse)
    return jnp.sum(kernel * source_charge[None, :], axis=1)


def pair_sums(target, target_labels, source, source_labels, source_charge, forces):
    count = target.shape[1]
    extent = source.shape[1]
    block = extent
    while block * count > pair_limit and block % 2 == 0:
        block = block // 2
    turns = extent // block
    source_blocks = source.reshape(4, turns, block).transpose(1, 0, 2)
    label_blocks = source_labels.reshape(turns, block)
    charge_blocks = source_charge.reshape(turns, block)
    start_value = jnp.zeros((9, count) if forces else (count,), jnp.float32)

    def accumulate(carry, item):
        return (carry + pair_block(target, target_labels, item[0], item[1], item[2], forces), None)

    total, _ = lax.scan(accumulate, start_value, (source_blocks, label_blocks, charge_blocks))
    return total


def edge_terms(receive, sender_rows, vectors, projected, w_rad1, w_rad2, atoms):
    length = jnp.sqrt(jnp.sum(vectors * vectors, axis=0))
    unit = vectors / length
    order = jnp.arange(1, w_rad1.shape[0] + 1, dtype=jnp.int32).astype(jnp.float32)[:, None]
    ratio = length / cutoff
    envelope = (1.0 - ratio * ratio) * (1.0 - ratio * ratio)
    basis = jnp.sin(order * math.pi * ratio) / ratio * envelope
    mixed = lax.dot_general(
        basis, w_rad1, (((0,), (0,)), ((), ())), precision=lax.Precision.HIGHEST
    )
    radial = jax.nn.silu(mixed).astype(jnp.bfloat16)
    filters = jnp.dot(radial, w_rad2, preferred_element_type=jnp.float32)
    picked = jnp.take(projected, sender_rows, axis=0).astype(jnp.float32) * filters
    chans = w_rad1.shape[1]
    scalar = picked[:, :chans]
    carried = picked[:, chans:]
    joined = [
        scalar,
        unit[0][:, None] * carried,
        unit[1][:, None] * carried,
        unit[2][:, None] * carried,
    ]
    message = jnp.concatenate(joined, axis=1).astype(jnp.bfloat16)
    onehot = (jnp.arange(atoms, dtype=jnp.int32)[:, None] == receive[None, :]).astype(jnp.bfloat16)
    return jnp.dot(onehot, message, preferred_element_type=jnp.float32)


def shards(
    features,
    positions,
    species,
    ghost_list,
    edge_recv,
    edge_send,
    edge_vec,
    w_msg,
    w_rad1,
    w_rad2,
    w_up,
    w_out,
    hardness,
    width,
    chi_shift,
    field,
):
    atoms = features.shape[0]
    chans = features.shape[1]
    lanes = lax.axis_size("space")
    row_at = lax.axis_index("row")
    space_at = lax.axis_index("space")
    lists = ghost_list[0]
    outgoing = jnp.take(features, lists.reshape(-1), axis=0).reshape(lanes, lists.shape[1], chans)
    ghost_rows = jnp.einsum(
        "dkc,cf->dkf",
        lax.all_to_all(outgoing, "space", split_axis=0, concat_axis=0, tiled=True),
        w_msg,
        preferred_element_type=jnp.float32,
    ).astype(jnp.bfloat16)
    own_rows = jnp.dot(features, w_msg, preferred_element_type=jnp.float32).astype(jnp.bfloat16)
    projected = jnp.concatenate([own_rows, ghost_rows.reshape(-1, 2 * chans)], axis=0)
    summed = edge_terms(edge_recv, edge_send, edge_vec, projected, w_rad1, w_rad2, atoms)
    summed = summed * message_scale
    vector_part = summed[:, chans:].reshape(atoms, 3, chans)
    invariant = jnp.concatenate(
        [summed[:, :chans], jnp.sum(vector_part * vector_part, axis=1)], axis=1
    ).astype(jnp.bfloat16)
    hidden = jax.nn.silu(jnp.dot(invariant, w_up, preferred_element_type=jnp.float32))
    new_features = (features.astype(jnp.float32) + hidden).astype(jnp.bfloat16)
    chi = jnp.dot(hidden, w_out, precision=lax.Precision.HIGHEST) + lookup(species, chi_shift)
    sigma = lookup(species, width)
    diag = lookup(species, hardness) + inverse_root_pi / sigma
    placed = jnp.concatenate([positions, sigma[None, :]], axis=0)
    own_labels = (row_at * lanes + space_at) * atoms + jnp.arange(atoms, dtype=jnp.int32)
    everyone = lax.all_gather(placed, ("row", "space"), axis=1, tiled=True)
    all_labels = jnp.arange(everyone.shape[1], dtype=jnp.int32)

    def spread_out(vector):
        return lax.all_gather(vector, ("row", "space"), axis=0, tiled=True)

    rhs = field[0] * positions[2] - chi
    charges = jnp.zeros_like(rhs)
    residual = rhs

    def squares(current):
        return lax.psum(jnp.sum(current * current), ("row", "space"))

    direction = residual
    norm_now = squares(residual)
    for step in range(ITERS):
        image = diag * direction + pair_sums(
            placed, own_labels, everyone, all_labels, spread_out(direction), False
        )
        alpha = norm_now / lax.psum(jnp.sum(direction * image), ("row", "space"))
        charges = charges + alpha * direction
        residual = residual - alpha * image
        fresh = squares(residual)
        direction = residual + fresh / norm_now * direction
        norm_now = fresh
    sums = pair_sums(placed, own_labels, everyone, all_labels, spread_out(charges), True)
    pull = -charges[None, :] * sums[:3]
    forces = jnp.concatenate([pull[:2], pull[2:] + (charges * field[0])[None, :]], axis=0)
    virial = 0.5 * charges[None, :] * sums[3:]
    return (new_features, charges, forces, virial)


def solution(mesh):
    return jax.shard_map(
        shards,
        mesh=mesh,
        in_specs=(
            P(("row", "space"), None),
            P(None, ("row", "space")),
            P(("row", "space")),
            P("row", "space", None),
            P(("row", "space")),
            P(("row", "space")),
            P(None, ("row", "space")),
            P(),
            P(),
            P(),
            P(),
            P(),
            P(),
            P(),
            P(),
            P(),
        ),
        out_specs=(
            P(("row", "space"), None),
            P(("row", "space")),
            P(None, ("row", "space")),
            P(None, ("row", "space")),
        ),
        check_vma=False,
    )
```

profile of v0, /device:TPU:1, one launch (start us, length us, event | category | flops | bytes accessed | tf_op | source)
XLA Modules:
  0.0 782.4 jit_solution(4420758810562936162)
XLA Ops:
  0.6 0.0 copy-start
  0.6 0.8 reshape_squeeze.6
  1.5 0.7 compare_and_fusion
  2.2 0.0 copy-start.5
  2.2 0.0 copy-start.6
  2.3 0.0 copy-start.7
  2.3 3.6 gather_fusion
  5.9 0.9 broadcast_select_fusion
  6.8 10.4 %all-to-all-start = ((bf16[32,32,128]{2,1,0:T(8,128)(2,1)}), bf16[32,32,128]{2,1,0:T(8,128)(2,1)S(1)}, u32[]{:S(2)}, u32[]{:S(2)}) async-start(bf16[32,32,128]{2,1,0:T(8,128)(2,1)} %broadcast_select_fusion), calls=%async_computation | async-start | bytes 524288 | tf_op jit(solution)/shard_map/all_to_all | solution.py:125
  18.0 0.7 fusion.42
  18.7 0.7 fusion.43
  19.3 0.6 fusion.44
  20.0 0.1 convolution_convert_fusion.1
  20.1 2.5 fusion.39
  22.7 138.5 %all-gather = f32[512,16,4]{1,2,0:T(4,128)S(1)} all-gather(f32[1,16,4]{1,2,0:T(4,128)S(1)} %maximum_bitcast_fusion), channel_id=1, replica_groups=mesh['row'=16,'space'=32] {'row','space'}, dimensions={0}, use_global_device_ids=true | all-gather | bytes 131328 | tf_op jit(solution)/shard_map/all_gather | solution.py:144
  161.2 0.1 copy.26
  161.2 0.6 reshape.216
  161.8 0.0 copy-done.12
  161.8 0.7 multiply_convert_fusion.3
  162.6 0.3 broadcast_subtract_fusion
  162.9 0.3 convolution_convert_fusion
  163.2 2.0 gather_fusion.1
  165.2 0.1 copy.25
  165.3 1.1 convolution_multiply_fusion
  166.5 0.1 multiply_convert_fusion.2
  166.5 0.2 convolution_multiply_fusion.1
  166.9 0.4 copy-done.2
  167.3 0.7 add_convert_fusion
  168.0 2.6 fusion.1
  170.6 0.3 dynamic-update-slice
  170.9 100.5 %all-reduce = f32[8192]{0:T(1024)S(1)} all-reduce(f32[8192]{0:T(1024)S(1)} %dynamic-update-slice), channel_id=1, replica_groups=mesh['row'=16,'space'=32] {'row','space'}, use_global_device_ids=true, to_apply=%add | all-reduce | flops 8192 | bytes 65536
  271.4 0.5 multiply_reduce_fusion.8
  271.9 3.2 multiply_reduce_fusion.12
  275.0 99.4 %all-reduce.3 = (f32[]{:T(128)}, f32[]{:T(128)}) all-reduce(f32[]{:T(128)} %get-tuple-element.67, f32[]{:T(128)} %get-tuple-element.66), channel_id=1, replica_groups=mesh['row'=16,'space'=32] {'row','space'}, use_global_device_ids=true, to_apply=%region_3.4 | all-reduce | flops 2 | bytes 16 | tf_op jit(solution)/shard_map/psum | solution.py:155
  375.8 0.6 multiply_reduce_fusion.11
  376.4 99.4 %psum.30 = f32[]{:T(128)} all-reduce(f32[]{:T(128)} %get-tuple-element.83), channel_id=1, replica_groups=mesh['row'=16,'space'=32] {'row','space'}, use_global_device_ids=true, to_apply=%region_9.10 | all-reduce | flops 1 | bytes 8 | tf_op jit(solution)/shard_map/psum | solution.py:155
  477.1 0.1 fusion.38
  477.2 100.3 %all-reduce.1 = f32[8192]{0:T(1024)S(1)} all-reduce(f32[8192]{0:T(1024)S(1)} %get-tuple-element.81), channel_id=1, replica_groups=mesh['row'=16,'space'=32] {'row','space'}, use_global_device_ids=true, to_apply=%add.1 | all-reduce | flops 8192 | bytes 65536
  577.5 0.3 multiply_reduce_fusion.7
  577.8 0.6 multiply_reduce_fusion.10
  578.4 99.4 %psum.31 = f32[]{:T(128)} all-reduce(f32[]{:T(128)} %multiply_reduce_fusion.10), channel_id=1, replica_groups=mesh['row'=16,'space'=32] {'row','space'}, use_global_device_ids=true, to_apply=%region_12.13 | all-reduce | flops 1 | bytes 8 | tf_op jit(solution)/shard_map/psum | solution.py:163
  679.3 0.3 dynamic-update-slice.2
  679.6 100.3 %all-reduce.2 = f32[8192]{0:T(1024)S(1)} all-reduce(f32[8192]{0:T(1024)S(1)} %dynamic-update-slice.2), channel_id=1, replica_groups=mesh['row'=16,'space'=32] {'row','space'}, use_global_device_ids=true, to_apply=%add.2 | all-reduce | flops 8192 | bytes 65536
  779.8 0.9 multiply_reduce_fusion.2
  780.7 0.4 multiply_reduce_fusion
  781.1 0.0 copy-done.11
  781.2 0.6 pad_maximum_fusion.1
  781.8 0.6 broadcast_multiply_fusion
  (52 shorter events, 0.4 us)
Async XLA Ops:
  0.6 19.3 %copy-start = (bf16[128,256]{1,0:T(8,128)(2,1)S(1)}, bf16[128,256]{1,0:T(8,128)(2,1)}, u32[]{:S(2)}) copy-start(bf16[128,256]{1,0:T(8,128)(2,1)} %param.23) | copy-start | bytes 196612
  2.2 15.0 %copy-start.5 = (s32[512]{0:T(512)S(1)}, s32[512]{0:T(512)}, u32[]{:S(2)}) copy-start(s32[512]{0:T(512)} %param.21) | copy-start | bytes 6148
  2.2 15.7 %copy-start.3 = (f32[3,512]{1,0:T(4,128)S(1)}, f32[3,512]{1,0:T(4,128)}, u32[]{:S(2)}) copy-start(f32[3,512]{1,0:T(4,128)} %param.22) | copy-start | bytes 18436
  2.2 15.8 %copy-start.6 = (f32[4]{0:T(128)S(1)}, f32[4]{0:T(128)}, u32[]{:S(2)}) copy-start(f32[4]{0:T(128)} %param.28) | copy-start | bytes 52
  2.3 16.4 %copy-start.7 = (f32[4]{0:T(128)S(1)}, f32[4]{0:T(128)}, u32[]{:S(2)}) copy-start(f32[4]{0:T(128)} %param.29) | copy-start | bytes 52
  2.3 17.1 %copy-start.8 = (f32[4]{0:T(128)S(1)}, f32[4]{0:T(128)}, u32[]{:S(2)}) copy-start(f32[4]{0:T(128)} %param.30) | copy-start | bytes 52
  2.3 17.7 %copy-start.1 = (bf16[16,128]{1,0:T(8,128)(2,1)S(1)}, bf16[16,128]{1,0:T(8,128)(2,1)}, u32[]{:S(2)}) copy-start(bf16[16,128]{1,0:T(8,128)(2,1)} %param.16) | copy-start | bytes 12292
  2.3 17.8 %copy-start.9 = (s32[16]{0:T(128)S(1)}, s32[16]{0:T(128)}, u32[]{:S(2)}) copy-start(s32[16]{0:T(128)} %param.18) | copy-start | bytes 196
  2.3 20.4 %copy-start.4 = (f32[3,16]{1,0:T(4,128)S(1)}, f32[3,16]{1,0:T(4,128)}, u32[]{:S(2)}) copy-start(f32[3,16]{1,0:T(4,128)} %param.17) | copy-start | bytes 580
  6.8 156.0 %all-to-all-start = ((bf16[32,32,128]{2,1,0:T(8,128)(2,1)}), bf16[32,32,128]{2,1,0:T(8,128)(2,1)S(1)}, u32[]{:S(2)}, u32[]{:S(2)}) async-start(bf16[32,32,128]{2,1,0:T(8,128)(2,1)} %broadcast_select_fusion), calls=%async_computation | async-start | bytes 524288 | tf_op jit(solution)/shard_map/all_to_all | solution.py:125
  161.2 0.7 copy-start.12
  165.1 1.4 copy-start.13
  166.4 0.8 copy-start.2
  166.4 1.6 copy-start.10
  166.4 1.6 copy-start.14
  679.2 101.9 %copy-start.11 = (f32[16]{0:T(128)}, f32[16]{0:T(128)S(1)}, u32[]{:S(2)}) copy-start(f32[16]{0:T(128)S(1)} %get-tuple-element.71) | copy-start | bytes 196
where the time goes:
time: 784 us; the launch traced here: 782 us
  blocking collectives  738 us (94%)
  other arithmetic  12.5 us (2%)
  starting transfers between devices  10.4 us (1%)
  local copies, waits for them, and re-layouts  10.2 us (1%)
    unnamed x3, blocking collectives  301 us
    psum x2, blocking collectives, squares(): return lax.psum(jnp.sum(current * current), ('row', 'space'))  199 us
    all_gather x1, blocking collectives, shards(): everyone = lax.all_gather(placed, ('row', 'space'), axis=1, tiled=True)  138 us
    psum x1, blocking collectives, shards(): alpha = norm_now / lax.psum(jnp.sum(direction * image), ('row', 'space'))  99.4 us
  transfers between devices with their start and end apart: 1, of which 0 were waited for; matrix products, arithmetic and copies ran while one was open for 1% of the time, Pallas kernels for 0%

commit v1 on v0

v1 whole, which is shorter than its diff:
```python
import functools
import math

import jax
import jax.numpy as jnp
from jax import lax
from jax.experimental import pallas as pl
from jax.experimental.pallas import tpu as pltpu
from jax.sharding import PartitionSpec as P

MESH = pl.DeviceIdType.MESH
NZ = 16
NS = 32
A = 16
L = 128
E = 512

CUTOFF = 6.0
MESSAGE_SCALE = 0.125
TWO_OVER_ROOT_PI = 2.0 / math.sqrt(math.pi)
INVERSE_ROOT_PI = 1.0 / math.sqrt(math.pi)

ERF_P = 0.45
ERF_C = (
    0.25898973,
    0.20100906,
    0.46017168,
    -0.37580456,
    0.85716943,
    -0.49410514,
    0.09256981,
)

X_LIST, X_FEAT, X_POS_Z, X_POS_P, X_B_Z, X_B_P, X_Y_Z, X_Y_P, X_S_Z, X_S_P = range(10)
EXCHANGES = 10

f32 = jnp.float32
bf16 = jnp.bfloat16


def iota(shape, dim):
    return lax.broadcasted_iota(jnp.int32, shape, dim)


def kernel(
    feat, pos, species, ghosts, recv, sender, evec, w_msg, w_rad1, w_rad2, w_up, w_out,
    hardness, width, chi_shift, field,
    nf_out, q_out, f_out, v_out,
    lists, list_in, feat_in, own_in, packet, zpos, line, ppos, zvec, pair, vecs, zsum, psum,
    fil, base, slot, first, columns, coords, green, slopes, part, rows9, send_sem, recv_sem,
):
    z = lax.axis_index("row")
    s = lax.axis_index("space")
    barrier = pltpu.get_barrier_semaphore()

    @pl.loop(1, NZ)
    def _(k):
        pl.semaphore_signal(
            barrier, inc=1, device_id=(lax.rem(z + k, NZ), s), device_id_type=MESH
        )

    @pl.loop(1, NS)
    def _(k):
        pl.semaphore_signal(
            barrier, inc=1, device_id=(z, lax.rem(s + k, NS)), device_id_type=MESH
        )

    def send_z(which, src, dst, rows):
        @pl.loop(1, NZ)
        def _(k):
            pltpu.make_async_remote_copy(
                src_ref=src,
                dst_ref=dst.at[pl.ds(z * rows, rows)],
                send_sem=send_sem.at[which],
                recv_sem=recv_sem.at[which],
                device_id=(lax.rem(z + k, NZ), s),
                device_id_type=MESH,
            ).start()

    def send_p(which, source, dst, rows):
        at = pl.multiple_of(s * rows, rows)

        @pl.loop(1, NS)
        def _(k):
            peer = lax.rem(s + k, NS)
            pltpu.make_async_remote_copy(
                src_ref=source(peer),
                dst_ref=dst.at[pl.ds(at, rows)],
                send_sem=send_sem.at[which],
                recv_sem=recv_sem.at[which],
                device_id=(z, peer),
                device_id_type=MESH,
            ).start()

    def await_rows(sem, dst, rows):
        some = dst.at[pl.ds(0, rows)]
        pltpu.make_async_copy(some, some, sem).wait()

    lane = iota((1, L), 1)
    half = z // 8
    off = lax.rem(z, 8) * A
    mine = (lane >= off) & (lane < off + A)
    diagonal = iota((A, L), 1) == iota((A, L), 0) + off

    def to_row(column):
        return jnp.sum(jnp.where(diagonal, column, 0.0), axis=0, keepdims=True)

    own_in[...] = jnp.zeros_like(own_in)
    own_in[0:3, 0:A] = pos[...]
    own_in[3:4, 0:A] = species[...].astype(f32)
    own = pltpu.roll(own_in[...], off, axis=1)
    kind = own[3:4]

    def lookup(table):
        out = jnp.zeros((1, L), f32)
        for k in range(4):
            out = out + jnp.where(mine & (kind == k), table[k], 0.0)
        return out

    sigma = jnp.where(mine, lookup(width), 1.0)
    diag = jnp.where(mine, lookup(hardness) + INVERSE_ROOT_PI / sigma, 0.0)
    packet[0:3, :] = own[0:3]
    packet[3:4, :] = jnp.where(mine, 2.0 * sigma * sigma, 0.0)
    packet[4:8, :] = jnp.zeros((4, L), f32)
    lists[...] = jnp.zeros_like(lists)
    lists[:, 0:NS] = ghosts[0]
    list_in[NS:, :] = jnp.zeros((L - NS, L), jnp.int32)

    vectors = evec[...]
    squared = vectors[0:1] * vectors[0:1] + vectors[1:2] * vectors[1:2] + vectors[2:3] * vectors[2:3]
    length = jnp.sqrt(squared)
    unit = vectors / length
    ratio = length / CUTOFF
    envelope = (1.0 - ratio * ratio) * (1.0 - ratio * ratio)
    order = (iota((8, 1), 0) + 1).astype(f32)
    basis = jnp.sin(order * math.pi * ratio) / ratio * envelope
    mixed = lax.dot_general(
        basis, w_rad1[...], (((0,), (0,)), ((), ())),
        precision=lax.Precision.HIGHEST, preferred_element_type=f32,
    )
    radial = jax.nn.silu(mixed).astype(bf16)
    filters = jnp.dot(radial, w_rad2[...], preferred_element_type=f32)
    slots = sender[...]
    local = slots < A
    ghost = slots - A
    columns[0:3, :] = unit
    columns[3:4, :] = jnp.where(local, s * A + slots, (ghost // NS) * A).astype(f32)
    columns[4:5, :] = jnp.where(local, -1, ghost // NS).astype(f32)
    columns[5:6, :] = lax.rem(jnp.where(local, 0, ghost), NS).astype(f32)
    columns[6:8, :] = jnp.zeros((2, E), f32)
    turned = columns[...].T
    fil[:, 0:L] = filters[:, 0:L]
    for c in range(3):
        fil[:, (c + 1) * L : (c + 2) * L] = filters[:, L:] * turned[:, c : c + 1]
    lane_f = iota((E, L), 1).astype(f32)
    base[...] = lane_f - turned[:, 3:4]
    first[...] = jnp.where(lane_f == turned[:, 4:5], 1.0, 0.0).astype(bf16)
    slot[...] = jnp.where(lane_f == turned[:, 5:6], 1.0, 0.0)
    receivers = jnp.where(iota((A, E), 0) == recv[...], 1.0, 0.0).astype(bf16)

    pl.semaphore_wait(barrier, NZ + NS - 2)
    send_p(X_LIST, lambda peer: lists.at[pl.ds(peer, 1)], list_in, 1)
    send_p(X_FEAT, lambda peer: feat, feat_in, A)
    send_z(X_POS_Z, packet.at[pl.ds(0, 4)], zpos, 4)
    list_in[pl.ds(s, 1), :] = lists[pl.ds(s, 1), :]
    feat_in[pl.ds(pl.multiple_of(s * A, A), A), :] = feat[...]
    zpos[pl.ds(z * 4, 4), :] = packet[0:4, :]

    await_rows(recv_sem.at[X_LIST], list_in, NS - 1)
    found = jnp.dot(first[...], list_in[...].astype(f32).astype(bf16), preferred_element_type=f32)
    found = (found * slot[...]).astype(bf16)
    found = jnp.dot(found, jnp.ones((L, L), bf16), preferred_element_type=f32)
    await_rows(recv_sem.at[X_FEAT], feat_in, (NS - 1) * A)
    offset = base[...] - found
    picks = jnp.concatenate(
        [jnp.where(offset == float(-L * g), 1.0, 0.0).astype(bf16) for g in range(4)], axis=1
    )
    picked = jnp.dot(picks, feat_in[...], preferred_element_type=f32).astype(bf16)
    projected = jnp.dot(picked, w_msg[...], preferred_element_type=f32).astype(bf16).astype(f32)
    lower, upper = projected[:, 0:L], projected[:, L:]
    message = jnp.concatenate(
        [(lower * fil[:, 0:L]).astype(bf16)]
        + [(upper * fil[:, (c + 1) * L : (c + 2) * L]).astype(bf16) for c in range(3)],
        axis=1,
    )
    summed = jnp.dot(receivers, message, preferred_element_type=f32) * MESSAGE_SCALE
    norms = summed[:, L : 2 * L] * summed[:, L : 2 * L]
    for c in range(2, 4):
        norms = norms + summed[:, c * L : (c + 1) * L] * summed[:, c * L : (c + 1) * L]
    invariant = jnp.concatenate([summed[:, 0:L], norms], axis=1).astype(bf16)
    hidden = jax.nn.silu(jnp.dot(invariant, w_up[...], preferred_element_type=f32))
    nf_out[...] = (feat[...].astype(f32) + hidden).astype(bf16)
    chi = to_row(jnp.sum(hidden * w_out[...], axis=1, keepdims=True)) + lookup(chi_shift)
    rhs = jnp.where(mine, field[0] * own[2:3] - chi, 0.0)

    def halves(k):
        return (
            jnp.sum(zvec[k, 0:8, :], axis=0, keepdims=True),
            jnp.sum(zvec[k, 8:16, :], axis=0, keepdims=True),
        )

    def start_gather(k, which, row):
        pair[k, 2:3, :] = row
        zvec[k, pl.ds(z, 1), :] = row
        send_z(which, pair.at[k, pl.ds(2, 1)], zvec.at[k], 1)

    def turn_gather(k, which, into):
        await_rows(recv_sem.at[which], zvec.at[k], NZ - 1)
        low, high = halves(k)
        pair[k, 0:1, :] = low
        pair[k, 1:2, :] = high
        send_p(into, lambda peer: pair.at[k, pl.ds(0, 2)], vecs.at[k], 2)
        vecs[k, pl.ds(2 * s, 1), :] = low
        vecs[k, pl.ds(2 * s + 1, 1), :] = high

    start_gather(0, X_B_Z, rhs)

    await_rows(recv_sem.at[X_POS_Z], zpos, (NZ - 1) * 4)
    for h in range(2):
        tiles = zpos[h * 32 : h * 32 + 8, :]
        for t in range(1, 4):
            tiles = tiles + zpos[h * 32 + 8 * t : h * 32 + 8 * t + 8, :]
        line[h * 4 : h * 4 + 4, :] = tiles[0:4] + tiles[4:8]
    send_p(X_POS_P, lambda peer: line, ppos, 8)
    ppos[pl.ds(pl.multiple_of(s * 8, 8), 8), :] = line[...]
    for h in range(2):
        for c in range(4):
            spread = jnp.broadcast_to(line[h * 4 + c : h * 4 + c + 1, :], (L, L))
            coords[c, h * L : (h + 1) * L, :] = spread.T

    turn_gather(0, X_B_Z, X_B_P)
    await_rows(recv_sem.at[X_POS_P], ppos, (NS - 1) * 8)
    where = [ppos[pl.ds(c, 64, stride=4), :] for c in range(4)]
    own_row = 2 * s + half

    @pl.loop(0, A)
    def _(i):
        at = [coords[c, pl.ds(z * A + i, 1), :] for c in range(4)]
        dx, dy, dz = (at[c] - where[c] for c in range(3))
        r2 = jnp.maximum(dx * dx + dy * dy + dz * dz, 1.0)
        inverse = lax.rsqrt(r2)
        scale = lax.rsqrt(at[3] + where[3])
        x = r2 * inverse * scale
        bell = jnp.exp(-x * x)
        t = 1.0 / (1.0 + ERF_P * x)
        poly = ERF_C[6]
        for c in ERF_C[5::-1]:
            poly = poly * t + c
        kernel_ij = (1.0 - bell * (poly * t)) * inverse
        green[i] = kernel_ij
        slopes[i] = inverse * inverse * (TWO_OVER_ROOT_PI * scale * bell - kernel_ij)
        green[i, pl.ds(own_row, 1), :] = jnp.where(
            lane == off + i, diag, green[i, pl.ds(own_row, 1), :]
        )

    def apply(vector):
        @pl.loop(0, A)
        def _(i):
            terms = green[i] * vector
            part[pl.ds(i, 1), :] = jnp.sum(terms, axis=0, keepdims=True)

        return to_row(jnp.sum(part[...], axis=1, keepdims=True))

    def total(value):
        return jnp.sum(jnp.sum(value, axis=0, keepdims=True), axis=1, keepdims=True)

    await_rows(recv_sem.at[X_B_P], vecs.at[0], (NS - 1) * 2)
    image = apply(vecs[0])
    start_gather(1, X_Y_Z, image)
    norm = total(vecs[0] * vecs[0])
    turn_gather(1, X_Y_Z, X_Y_P)
    await_rows(recv_sem.at[X_Y_P], vecs.at[1], (NS - 1) * 2)
    alpha = norm / total(vecs[0] * vecs[1])
    residual = vecs[0] - alpha * vecs[1]
    fresh = total(residual * residual)
    beta = fresh / norm
    vecs[2] = residual + beta * vecs[0]
    vecs[3] = alpha * vecs[0]
    step_row = (rhs - alpha * image) + beta * rhs
    second_image = apply(vecs[2])
    row = step_row * second_image
    pair[2, 2:3, :] = row
    zsum[pl.ds(z, 1), :] = row
    send_z(X_S_Z, pair.at[2, pl.ds(2, 1)], zsum, 1)

    def moments(part_id):
        @pl.loop(0, A)
        def _(i):
            at = [coords[c, pl.ds(z * A + i, 1), :] for c in range(3)]
            dx, dy, dz = (at[c] - where[c] for c in range(3))
            for v in range(2):
                weight = slopes[i] * vecs[3 - v]
                mx, my, mz = weight * dx, weight * dy, weight * dz
                outs = (mx, my, mz, mx * dx, my * dy, mz * dz, mx * dy, mx * dz, my * dz)
                for c, terms in enumerate(outs):
                    rows9[v, c, pl.ds(i, 1), :] = jnp.sum(terms, axis=0, keepdims=True)

    await_rows(recv_sem.at[X_S_Z], zsum, NZ - 1)
    row = jnp.sum(zsum[...], axis=0, keepdims=True)
    pair[3, 2:3, :] = row
    psum[pl.ds(s, 1), :] = row
    send_p(X_S_P, lambda peer: pair.at[3, pl.ds(2, 1)], psum, 1)
    moments(0)
    sums = [
        [to_row(jnp.sum(rows9[v, c], axis=1, keepdims=True)) for c in range(9)] for v in range(2)
    ]
    await_rows(recv_sem.at[X_S_P], psum, NS - 1)
    second_alpha = fresh / total(psum[...])
    charge = alpha * rhs + second_alpha * step_row
    moment = [sums[0][c] + second_alpha * sums[1][c] for c in range(9)]
    result = [charge]
    for c in range(3):
        force = -charge * moment[c]
        result.append(force + charge * field[0] if c == 2 else force)
    for c in range(3, 9):
        result.append(0.5 * charge * moment[c])
    result = jnp.concatenate(result + [jnp.zeros((6, L), f32)], axis=0)
    result = pltpu.roll(result, lax.rem(L - off, L), axis=1)
    q_out[...] = result[0:1, 0:A]
    f_out[...] = result[1:4, 0:A]
    v_out[...] = result[4:10, 0:A]

    for which, dst, rows in (
        (X_LIST, list_in, NS - 1),
        (X_FEAT, feat_in, (NS - 1) * A),
        (X_POS_Z, zpos, (NZ - 1) * 4),
        (X_POS_P, ppos, (NS - 1) * 8),
        (X_B_Z, zvec.at[0], NZ - 1),
        (X_B_P, vecs.at[0], (NS - 1) * 2),
        (X_Y_Z, zvec.at[1], NZ - 1),
        (X_Y_P, vecs.at[1], (NS - 1) * 2),
        (X_S_Z, zsum, NZ - 1),
        (X_S_P, psum, NS - 1),
    ):
        await_rows(send_sem.at[which], dst, rows)


def shards(
    features, positions, species, ghost_list, edge_recv, edge_send, edge_vec,
    w_msg, w_rad1, w_rad2, w_up, w_out, hardness, width, chi_shift, field,
):
    vmem = pl.BlockSpec(memory_space=pltpu.VMEM)
    smem = pl.BlockSpec(memory_space=pltpu.SMEM)
    new_features, charges, forces, virial = pl.pallas_call(
        kernel,
        out_shape=(
            jax.ShapeDtypeStruct((A, L), bf16),
            jax.ShapeDtypeStruct((1, A), f32),
            jax.ShapeDtypeStruct((3, A), f32),
            jax.ShapeDtypeStruct((6, A), f32),
        ),
        in_specs=[vmem] * 12 + [smem] * 4,
        out_specs=[vmem] * 4,
        scratch_shapes=[
            pltpu.VMEM((NS, L), jnp.int32),
            pltpu.VMEM((L, L), jnp.int32),
            pltpu.VMEM((NS * A, L), bf16),
            pltpu.VMEM((8, L), f32),
            pltpu.VMEM((8, L), f32),
            pltpu.VMEM((NZ * 4, L), f32),
            pltpu.VMEM((8, L), f32),
            pltpu.VMEM((NS * 8, L), f32),
            pltpu.VMEM((2, NZ, L), f32),
            pltpu.VMEM((4, 8, L), f32),
            pltpu.VMEM((4, 2 * NS, L), f32),
            pltpu.VMEM((NZ, L), f32),
            pltpu.VMEM((NS, L), f32),
            pltpu.VMEM((E, 4 * L), f32),
            pltpu.VMEM((E, L), f32),
            pltpu.VMEM((E, L), f32),
            pltpu.VMEM((E, L), bf16),
            pltpu.VMEM((8, E), f32),
            pltpu.VMEM((4, 2 * L, L), f32),
            pltpu.VMEM((A, 2 * NS, L), f32),
            pltpu.VMEM((A, 2 * NS, L), f32),
            pltpu.VMEM((A, L), f32),
            pltpu.VMEM((2, 9, A, L), f32),
            pltpu.SemaphoreType.DMA((EXCHANGES,)),
            pltpu.SemaphoreType.DMA((EXCHANGES,)),
        ],
        compiler_params=pltpu.CompilerParams(
            collective_id=0, has_side_effects=True, vmem_limit_bytes=32 * 1024 * 1024
        ),
    )(
        features, positions, species.reshape(1, A), ghost_list,
        edge_recv.reshape(1, E), edge_send.reshape(1, E), edge_vec,
        w_msg, w_rad1, w_rad2, w_up, w_out.reshape(1, L), hardness, width, chi_shift, field,
    )
    return new_features, charges.reshape(A), forces, virial


def solution(mesh):
    atoms = P(("row", "space"))
    columns = P(None, ("row", "space"))
    return jax.shard_map(
        shards,
        mesh=mesh,
        in_specs=(
            P(("row", "space"), None), columns, atoms, P("row", "space", None), atoms, atoms, columns,
        )
        + (P(),) * 9,
        out_specs=(P(("row", "space"), None), atoms, columns, columns),
        check_vma=False,
    )
```

time: 784 us -> 72 us (0.09)
  blocking collectives: 738 us -> 0 us
  Pallas kernels: 0 us -> 58.5 us
  other arithmetic: 12.5 us -> 0 us
  starting transfers between devices: 10.4 us -> 0 us
    unnamed x3 -> x0, blocking collectives: 301 us -> none
    psum x3 -> x0, blocking collectives: 298 us -> none  [the longest x2 199 us: squares(): return lax.psum(jnp.sum(current * current), ('row', 'space'))]
    all_gather x1 -> x0, blocking collectives: 138 us -> none  [shards(): everyone = lax.all_gather(placed, ('row', 'space'), axis=1, tiled=True)]
    pallas_call x0 -> x1, Pallas kernels: none -> 58.5 us  [shards(): pl.pallas_call(kernel, out_shape=(jax.ShapeDtypeStruct((A, L), bf16), jax...]
    all_to_all x1 -> x0, starting transfers between devices: 10.4 us -> none  [shards(): lax.all_to_all(outgoing, 'space', split_axis=0, concat_axis=0, tiled=True)]
    unnamed x36 -> x34, local copies, waits for them, and re-layouts: 1.62 us -> 11.5 us
  transfers between devices with their start and end apart: 1 -> 0, of which waited for: 0 -> 0; matrix products, arithmetic and copies ran while one was open for 1% -> 0% of each run, Pallas kernels for 0% -> 0%
where the time goes in v1:
time: 72 us; the launch traced here: 71.4 us
  Pallas kernels  58.5 us (81%)
  local copies, waits for them, and re-layouts  11.5 us (16%)
  between operations  1.34 us (2%)
    pallas_call x1, Pallas kernels, shards(): pl.pallas_call(kernel, out_shape=(jax.ShapeDtypeStruct((A, L), bf16), jax...  58.5 us
    unnamed x34, local copies, waits for them, and re-layouts  11.5 us

profile of v1, /device:TPU:1, one launch (start us, length us, event | category | flops | bytes accessed | tf_op | source)
XLA Modules:
  0.0 71.4 jit_solution(14179240207485175277)
XLA Ops:
  0.6 0.0 copy-start.4
  1.3 0.0 copy-start.10
  1.3 0.0 copy-start.11
  1.3 0.0 copy-done.4
  1.3 0.6 copy-done.10
  2.0 0.0 copy-done.11
  2.0 0.0 copy-start
  2.0 0.8 %copy-done = bf16[128,256]{1,0:T(8,128)(2,1)S(1)} copy-done((bf16[128,256]{1,0:T(8,128)(2,1)S(1)}, bf16[128,256]{1,0:T(8,128)(2,1)}, u32[]{:S(2)}) %copy-start) | copy-done | bytes 65560
  2.8 0.0 copy-start.1
  2.8 0.8 %copy-done.1 = bf16[128,256]{1,0:T(8,128)(2,1)S(1)} copy-done((bf16[128,256]{1,0:T(8,128)(2,1)S(1)}, bf16[128,256]{1,0:T(8,128)(2,1)}, u32[]{:S(2)}) %copy-start.1) | copy-done | bytes 65560
  3.7 0.0 copy-start.2
  3.7 0.8 %copy-done.2 = bf16[256,128]{1,0:T(8,128)(2,1)S(1)} copy-done((bf16[256,128]{1,0:T(8,128)(2,1)S(1)}, bf16[256,128]{1,0:T(8,128)(2,1)}, u32[]{:S(2)}) %copy-start.2) | copy-done | bytes 65560
  4.5 0.0 copy-start.3
  4.5 0.7 %copy-done.3 = s32[1,32,32]{2,1,0:T(8,128)S(1)} copy-done((s32[1,32,32]{2,1,0:T(8,128)S(1)}, s32[1,32,32]{2,1,0:T(8,128)}, u32[]{:S(2)}) %copy-start.3) | copy-done | bytes 4120
  5.2 0.0 copy-start.5
  5.2 0.7 copy-done.5
  5.9 0.0 copy-start.6
  5.9 0.7 copy-done.6
  6.6 0.0 copy-start.7
  6.6 0.7 copy-done.7
  7.3 0.0 copy-start.8
  7.3 0.7 copy-done.8
  8.0 0.0 copy-start.9
  8.0 0.7 copy-done.9
  8.6 0.0 copy-start.12
  8.6 0.7 copy-done.12
  9.3 0.0 copy-start.13
  9.3 0.7 copy-done.13
  9.9 0.0 copy-start.14
  10.0 0.7 copy-done.14
  10.6 58.5 %shard_map.183 = (bf16[16,128]{1,0:T(8,128)(2,1)S(1)}, f32[1,16]{1,0:T(1,128)S(1)}, f32[3,16]{1,0:T(4,128)S(1)}, f32[6,16]{1,0:T(8,128)S(1)}) custom-call(bf16[16,128]{1,0:T(8,128)(2,1)S(1)} %copy-done.5, f32[3,16]{1,0:T(4,128)S(1)} %copy-done.7, s32[1,16]{1,0:T(1,128)S(1)} %bitcast.7, s32[1,32,32]{2,1,0:T(8,128)S(1)} %copy-done.3, s32[1,512]{1,0:T(1,128)S(1)} %bitcast.5, ...), custom_call_target="tpu_custom_call" | custom-call | tf_op jit(solution)/shard_map/pallas_call | solution.py:344
  69.2 0.6 copy.25
  69.7 0.5 copy.26
  70.3 0.6 copy.27
  70.8 0.6 copy.28
Async XLA Ops:
  0.6 0.7 copy-start.4
  1.3 0.7 copy-start.10
  1.3 0.7 copy-start.11
  2.0 0.8 %copy-start = (bf16[128,256]{1,0:T(8,128)(2,1)S(1)}, bf16[128,256]{1,0:T(8,128)(2,1)}, u32[]{:S(2)}) copy-start(bf16[128,256]{1,0:T(8,128)(2,1)} %w_msg.1) | copy-start | bytes 196612
  2.8 0.8 %copy-start.1 = (bf16[128,256]{1,0:T(8,128)(2,1)S(1)}, bf16[128,256]{1,0:T(8,128)(2,1)}, u32[]{:S(2)}) copy-start(bf16[128,256]{1,0:T(8,128)(2,1)} %w_rad2.1) | copy-start | bytes 196612
  3.7 0.8 %copy-start.2 = (bf16[256,128]{1,0:T(8,128)(2,1)S(1)}, bf16[256,128]{1,0:T(8,128)(2,1)}, u32[]{:S(2)}) copy-start(bf16[256,128]{1,0:T(8,128)(2,1)} %w_up.1) | copy-start | bytes 196612
  4.5 0.7 %copy-start.3 = (s32[1,32,32]{2,1,0:T(8,128)S(1)}, s32[1,32,32]{2,1,0:T(8,128)}, u32[]{:S(2)}) copy-start(s32[1,32,32]{2,1,0:T(8,128)} %ghosts.1) | copy-start | bytes 12292
  5.2 0.7 copy-start.5
  5.9 0.7 copy-start.6
  6.6 0.7 copy-start.7
  7.3 0.7 copy-start.8
  8.0 0.7 copy-start.9
  8.6 0.7 copy-start.12
  9.3 0.7 copy-start.13
  9.9 0.7 copy-start.14

commit v2 on v1

v2 whole, which is shorter than its diff:
```python
import functools
import math

import jax
import jax.numpy as jnp
from jax import lax
from jax.experimental import pallas as pl
from jax.experimental.pallas import tpu as pltpu
from jax.sharding import PartitionSpec as P

MESH = pl.DeviceIdType.MESH
NZ = 16
NS = 32
A = 16
L = 128
E = 512

CUTOFF = 6.0
MESSAGE_SCALE = 0.125
TWO_OVER_ROOT_PI = 2.0 / math.sqrt(math.pi)
INVERSE_ROOT_PI = 1.0 / math.sqrt(math.pi)

ERF_P = 0.55
ERF_C = (0.30158329, 0.39084308, -0.04142873, 0.75971775, -0.51804038, 0.10732501)

X_LIST, X_FEAT, X_POS_Z, X_B_Z, X_B_P, X_Y, X_S, X_POS_P = range(8)
GROUPS = 8
EXCHANGES = X_POS_P + GROUPS
GROUP_ORDER = (0, 2, 6, 1, 4, 3, 7, 5)
EARLY = 4

f32 = jnp.float32
bf16 = jnp.bfloat16


def iota(shape, dim):
    return lax.broadcasted_iota(jnp.int32, shape, dim)


def reciprocal(x):
    guess = pl.reciprocal(x, approx=True)
    return guess * (2.0 - x * guess)


def smeared(r2, spread):
    inverse = lax.rsqrt(r2)
    scale = lax.rsqrt(spread)
    x = r2 * inverse * scale
    bell = jnp.exp(-(x * x))
    t = reciprocal(1.0 + ERF_P * x)
    poly = ERF_C[5]
    for c in ERF_C[4::-1]:
        poly = poly * t + c
    return (1.0 - bell * (poly * t)) * inverse, TWO_OVER_ROOT_PI * scale * bell, inverse


def kernel(*refs):
    given = refs[:16]
    nf_out, result_out = refs[16:18]
    held = refs[18:34]
    (
        lists, list_in, feat_in, own_in, packet, zpos, line, ppos, zvec, pair, vecs, psum,
        fil, base, slot, first, columns, coords, own_at, green, part, rows9,
        send_sem, recv_sem, in_sem,
    ) = refs[34:]
    (
        feat, pos, species, ghosts, recv, sender, evec, w_msg, w_rad1, w_rad2, w_up, w_out,
        hardness, width, chi_shift, field,
    ) = held
    z = lax.axis_index("row")
    s = lax.axis_index("space")
    twin = z + 1 - 2 * lax.rem(z, 2)
    barrier = pltpu.get_barrier_semaphore()

    def signal(device):
        pl.semaphore_signal(barrier, inc=1, device_id=device, device_id_type=MESH)

    @pl.loop(1, NZ)
    def _(k):
        signal((lax.rem(z + k, NZ), s))

    @pl.loop(1, NS)
    def _(k):
        signal((z, lax.rem(s + k, NS)))
        signal((twin, lax.rem(s + k, NS)))

    loads = [pltpu.make_async_copy(given[k], held[k], in_sem.at[k]) for k in range(16)]
    for load in loads:
        load.start()

    def send(which, source, destination, device):
        pltpu.make_async_remote_copy(
            src_ref=source,
            dst_ref=destination,
            send_sem=send_sem.at[which],
            recv_sem=recv_sem.at[which],
            device_id=device,
            device_id_type=MESH,
        ).start()

    def send_z(which, src, dst, rows):
        @pl.loop(1, NZ)
        def _(k):
            send(which, src, dst.at[pl.ds(z * rows, rows)], (lax.rem(z + k, NZ), s))

    def send_p(which, source, dst, rows):
        at = pl.multiple_of(s * rows, rows)

        @pl.loop(1, NS)
        def _(k):
            peer = lax.rem(s + k, NS)
            send(which, source(peer), dst.at[pl.ds(at, rows)], (z, peer))

    def send_two_planes(which, src, dst, at):
        send(which, src, dst.at[pl.ds(at, 1)], (twin, s))

        @pl.loop(1, NS)
        def _(k):
            peer = lax.rem(s + k, NS)
            send(which, src, dst.at[pl.ds(at, 1)], (twin, peer))
            send(which, src, dst.at[pl.ds(at, 1)], (z, peer))

    def await_rows(sem, dst, rows):
        some = dst.at[pl.ds(0, rows)]
        pltpu.make_async_copy(some, some, sem).wait()

    lane = iota((1, L), 1)
    half = z // 8
    off = lax.rem(z, 8) * A
    mine = (lane >= off) & (lane < off + A)
    diagonal = iota((A, L), 1) == iota((A, L), 0) + off
    chunk = lax.rem(z, 2)

    def to_row(column):
        return jnp.sum(jnp.where(diagonal, column, 0.0), axis=0, keepdims=True)

    for load in loads:
        load.wait()
    own_in[...] = jnp.zeros_like(own_in)
    own_in[0:3, 0:A] = pos[...]
    own_in[3:4, 0:A] = species[...].astype(f32)
    own = pltpu.roll(own_in[...], off, axis=1)
    kind = own[3:4]

    def lookup(table):
        out = jnp.zeros((1, L), f32)
        for k in range(4):
            out = out + jnp.where(mine & (kind == k), table[k], 0.0)
        return out

    sigma = jnp.where(mine, lookup(width), 1.0)
    spread = jnp.where(mine, 2.0 * sigma * sigma, 0.0)
    packet[0:3, :] = own[0:3]
    packet[3:4, :] = spread
    packet[4:5, :] = jnp.where(mine, lookup(hardness) + INVERSE_ROOT_PI / sigma, 0.0)
    packet[5:8, :] = jnp.zeros((3, L), f32)
    for c in range(4):
        column = jnp.sum(jnp.where(diagonal, packet[c : c + 1, :], 0.0), axis=1, keepdims=True)
        own_at[c] = jnp.broadcast_to(column, (A, L))
    lists[...] = jnp.zeros_like(lists)
    lists[:, 0:NS] = ghosts[0]
    list_in[NS:, :] = jnp.zeros((L - NS, L), jnp.int32)

    vectors = evec[...]
    squared = vectors[0:1] * vectors[0:1] + vectors[1:2] * vectors[1:2] + vectors[2:3] * vectors[2:3]
    length = jnp.sqrt(squared)
    unit = vectors / length
    ratio = length / CUTOFF
    envelope = (1.0 - ratio * ratio) * (1.0 - ratio * ratio)
    order = (iota((8, 1), 0) + 1).astype(f32)
    basis = jnp.sin(order * math.pi * ratio) / ratio * envelope
    mixed = lax.dot_general(
        basis, w_rad1[...], (((0,), (0,)), ((), ())),
        precision=lax.Precision.HIGHEST, preferred_element_type=f32,
    )
    radial = jax.nn.silu(mixed).astype(bf16)
    filters = jnp.dot(radial, w_rad2[...], preferred_element_type=f32)
    slots = sender[...]
    local = slots < A
    ghost = slots - A
    columns[0:3, :] = unit
    columns[3:4, :] = jnp.where(local, s * A + slots, (ghost // NS) * A).astype(f32)
    columns[4:5, :] = jnp.where(local, -1, ghost // NS).astype(f32)
    columns[5:6, :] = lax.rem(jnp.where(local, 0, ghost), NS).astype(f32)
    columns[6:8, :] = jnp.zeros((2, E), f32)
    turned = columns[...].T
    fil[:, 0:L] = filters[:, 0:L]
    for c in range(3):
        fil[:, (c + 1) * L : (c + 2) * L] = filters[:, L:] * turned[:, c : c + 1]
    lane_f = iota((E, L), 1).astype(f32)
    base[...] = lane_f - turned[:, 3:4]
    first[...] = jnp.where(lane_f == turned[:, 4:5], 1.0, 0.0).astype(bf16)
    slot[...] = jnp.where(lane_f == turned[:, 5:6], 1.0, 0.0)
    receivers = jnp.where(iota((A, E), 0) == recv[...], 1.0, 0.0).astype(bf16)

    pl.semaphore_wait(barrier, NZ + 2 * NS - 3)
    send_p(X_LIST, lambda peer: lists.at[pl.ds(peer, 1)], list_in, 1)
    send_p(X_FEAT, lambda peer: feat, feat_in, A)
    send_z(X_POS_Z, packet, zpos, 8)
    list_in[pl.ds(s, 1), :] = lists[pl.ds(s, 1), :]
    feat_in[pl.ds(pl.multiple_of(s * A, A), A), :] = feat[...]
    zpos[pl.ds(pl.multiple_of(z * 8, 8), 8), :] = packet[...]

    await_rows(recv_sem.at[X_LIST], list_in, NS - 1)
    found = jnp.dot(first[...], list_in[...].astype(f32).astype(bf16), preferred_element_type=f32)
    found = (found * slot[...]).astype(bf16)
    found = jnp.dot(found, jnp.ones((L, L), bf16), preferred_element_type=f32)
    await_rows(recv_sem.at[X_FEAT], feat_in, (NS - 1) * A)
    offset = base[...] - found
    picks = jnp.concatenate(
        [jnp.where(offset == float(-L * g), 1.0, 0.0).astype(bf16) for g in range(4)], axis=1
    )
    picked = jnp.dot(picks, feat_in[...], preferred_element_type=f32).astype(bf16)
    projected = jnp.dot(picked, w_msg[...], preferred_element_type=f32).astype(bf16).astype(f32)
    lower, upper = projected[:, 0:L], projected[:, L:]
    message = jnp.concatenate(
        [(lower * fil[:, 0:L]).astype(bf16)]
        + [(upper * fil[:, (c + 1) * L : (c + 2) * L]).astype(bf16) for c in range(3)],
        axis=1,
    )
    summed = jnp.dot(receivers, message, preferred_element_type=f32) * MESSAGE_SCALE
    norms = summed[:, L : 2 * L] * summed[:, L : 2 * L]
    for c in range(2, 4):
        norms = norms + summed[:, c * L : (c + 1) * L] * summed[:, c * L : (c + 1) * L]
    invariant = jnp.concatenate([summed[:, 0:L], norms], axis=1).astype(bf16)
    hidden = jax.nn.silu(jnp.dot(invariant, w_up[...], preferred_element_type=f32))
    nf_out[...] = (feat[...].astype(f32) + hidden).astype(bf16)
    chi = to_row(jnp.sum(hidden * w_out[...], axis=1, keepdims=True)) + lookup(chi_shift)
    rhs = jnp.where(mine, field[0] * own[2:3] - chi, 0.0)

    pair[2:3, :] = rhs
    zvec[pl.ds(z, 1), :] = rhs
    send_z(X_B_Z, pair.at[pl.ds(2, 1)], zvec, 1)

    await_rows(recv_sem.at[X_POS_Z], zpos, (NZ - 1) * 8)
    for h in range(2):
        tile = zpos[h * 64 : h * 64 + 8, :]
        for t in range(1, 8):
            tile = tile + zpos[h * 64 + 8 * t : h * 64 + 8 * t + 8, :]
        line[h * 4 : h * 4 + 4, :] = tile[0:4]
        line[8 + h : 9 + h, :] = tile[4:5]
    own_group = s // 4

    @pl.loop(1, NS)
    def _(k):
        peer = lax.rem(s + k, NS)
        send(
            X_POS_P + own_group, line.at[pl.ds(0, 8)],
            ppos.at[pl.ds(pl.multiple_of(s * 8, 8), 8)], (z, peer),
        )

    ppos[pl.ds(pl.multiple_of(s * 8, 8), 8), :] = line[0:8, :]
    for c in range(4):
        spread_out = jnp.broadcast_to(line[pl.ds(chunk * 4 + c, 1), :], (L, L))
        coords[c] = spread_out.T
    diag_row = line[pl.ds(8 + chunk, 1), :]
    own_at_row = lax.rem(2 * s + chunk, 8)

    def fill(turn):
        group = own_group ^ GROUP_ORDER[turn]
        await_rows(recv_sem.at[X_POS_P + group], ppos, (3 if turn == 0 else 4) * 8)
        xs = [ppos[pl.ds(group * 32 + c, 8, stride=4), :] for c in range(4)]
        at_row = pl.multiple_of(group * 8, 8)

        @pl.loop(0, L, step=8)
        def _(i0):
            for i in range(8):
                at = [coords[c, pl.ds(i0 + i, 1), :] for c in range(4)]
                dx, dy, dz = (at[c] - xs[c] for c in range(3))
                r2 = jnp.maximum(dx * dx + dy * dy + dz * dz, 1.0)
                value = smeared(r2, at[3] + xs[3])[0]
                if turn == 0:
                    itself = (iota((8, L), 0) == own_at_row) & (iota((8, L), 1) == i0 + i)
                    value = jnp.where(itself, diag_row, value)
                green[i0 + i, pl.ds(at_row, 8), :] = value

    for turn in range(EARLY):
        fill(turn)
    await_rows(recv_sem.at[X_B_Z], zvec, NZ - 1)
    low = jnp.sum(zvec[0:8, :], axis=0, keepdims=True)
    high = jnp.sum(zvec[8:16, :], axis=0, keepdims=True)
    pair[0:1, :] = low
    pair[1:2, :] = high
    send_p(X_B_P, lambda peer: pair.at[pl.ds(0, 2)], vecs.at[0], 2)
    vecs[0, pl.ds(2 * s, 1), :] = low
    vecs[0, pl.ds(2 * s + 1, 1), :] = high
    for turn in range(EARLY, GROUPS):
        fill(turn)

    chunk_row = 2 * s + chunk

    def apply(vector):
        @pl.loop(0, L, step=4)
        def _(i0):
            for i in range(4):
                terms = green[i0 + i] * vector
                part[pl.ds(i0 + i, 1), :] = jnp.sum(terms, axis=0, keepdims=True)

        return jnp.sum(part[...].T, axis=0, keepdims=True)

    def total(value):
        return jnp.sum(jnp.sum(value, axis=0, keepdims=True), axis=1, keepdims=True)

    await_rows(recv_sem.at[X_B_P], vecs.at[0], (NS - 1) * 2)
    rhs_all = vecs[0]
    image = apply(rhs_all)
    pair[3:4, :] = image
    vecs[1, pl.ds(chunk_row, 1), :] = image
    send_two_planes(X_Y, pair.at[pl.ds(3, 1)], vecs.at[1], chunk_row)
    norm = total(rhs_all * rhs_all)
    await_rows(recv_sem.at[X_Y], vecs.at[1], 2 * NS - 1)
    image_all = vecs[1]
    alpha = norm / total(rhs_all * image_all)
    residual = rhs_all - alpha * image_all
    fresh = total(residual * residual)
    beta = fresh / norm
    vecs[2] = residual + beta * rhs_all
    vecs[3] = alpha * rhs_all
    row = vecs[2, pl.ds(chunk_row, 1), :] * apply(vecs[2])
    pair[4:5, :] = row
    psum[pl.ds(chunk_row, 1), :] = row
    send_two_planes(X_S, pair.at[pl.ds(4, 1)], psum, chunk_row)

    where = [ppos[pl.ds(c, 64, stride=4), :] for c in range(4)]

    @pl.loop(0, A)
    def _(i):
        at = [own_at[c, pl.ds(i, 1), :] for c in range(4)]
        dx, dy, dz = (at[c] - where[c] for c in range(3))
        r2 = jnp.maximum(dx * dx + dy * dy + dz * dz, 1.0)
        value, peak, inverse = smeared(r2, at[3] + where[3])
        slope = inverse * inverse * (peak - value)
        for v in range(2):
            weight = slope * vecs[3 - v]
            mx, my, mz = weight * dx, weight * dy, weight * dz
            outs = (mx, my, mz, mx * dx, my * dy, mz * dz, mx * dy, mx * dz, my * dz)
            for c, terms in enumerate(outs):
                rows9[v, c, pl.ds(i, 1), :] = jnp.sum(terms, axis=0, keepdims=True)

    sums = [
        [to_row(jnp.sum(rows9[v, c], axis=1, keepdims=True)) for c in range(9)] for v in range(2)
    ]
    own_row = 2 * s + half
    await_rows(recv_sem.at[X_S], psum, 2 * NS - 1)
    second_alpha = fresh / total(psum[...])
    charge = vecs[3, pl.ds(own_row, 1), :] + second_alpha * vecs[2, pl.ds(own_row, 1), :]
    moment = [sums[0][c] + second_alpha * sums[1][c] for c in range(9)]
    result = []
    for c in range(3):
        force = -charge * moment[c]
        result.append(force + charge * field[0] if c == 2 else force)
    result.append(charge)
    result.append(jnp.zeros((4, L), f32))
    for c in range(3, 9):
        result.append(0.5 * charge * moment[c])
    result.append(jnp.zeros((2, L), f32))
    result = jnp.concatenate(result, axis=0)
    result_out[...] = pltpu.roll(result, lax.rem(L - off, L), axis=1)

    for which, dst, rows in (
        (X_LIST, list_in, NS - 1),
        (X_FEAT, feat_in, (NS - 1) * A),
        (X_POS_Z, zpos, (NZ - 1) * 8),
        (X_POS_P + own_group, ppos, (NS - 1) * 8),
        (X_B_Z, zvec, NZ - 1),
        (X_B_P, vecs.at[0], (NS - 1) * 2),
        (X_Y, vecs.at[1], 2 * NS - 1),
        (X_S, psum, 2 * NS - 1),
    ):
        await_rows(send_sem.at[which], dst, rows)


def hand_out(nf, result, nf_out, q_out, f_out, v_out, q, f, v, sem):
    q[...] = result[3:4, 0:A]
    f[...] = result[0:3, 0:A]
    v[...] = result[8:14, 0:A]
    copies = [
        pltpu.make_async_copy(a, b, sem.at[k])
        for k, (a, b) in enumerate(((nf, nf_out), (q, q_out), (f, f_out), (v, v_out)))
    ]
    for copy in copies:
        copy.start()
    for copy in copies:
        copy.wait()


def shards(*given):
    given = list(given)
    for k, shape in ((2, (1, A)), (4, (1, E)), (5, (1, E)), (11, (1, L))):
        given[k] = given[k].reshape(shape)
    vmem = pl.BlockSpec(memory_space=pltpu.VMEM)
    hbm = pl.BlockSpec(memory_space=pltpu.HBM)
    held = [pltpu.VMEM(x.shape, x.dtype) for x in given[:12]]
    held += [pltpu.SMEM(x.shape, x.dtype) for x in given[12:]]
    new_features, result = pl.pallas_call(
        kernel,
        out_shape=(jax.ShapeDtypeStruct((A, L), bf16), jax.ShapeDtypeStruct((16, L), f32)),
        in_specs=[hbm] * 16,
        out_specs=[vmem] * 2,
        scratch_shapes=held
        + [
            pltpu.VMEM((NS, L), jnp.int32),
            pltpu.VMEM((L, L), jnp.int32),
            pltpu.VMEM((NS * A, L), bf16),
            pltpu.VMEM((8, L), f32),
            pltpu.VMEM((8, L), f32),
            pltpu.VMEM((NZ * 8, L), f32),
            pltpu.VMEM((16, L), f32),
            pltpu.VMEM((NS * 8, L), f32),
            pltpu.VMEM((NZ, L), f32),
            pltpu.VMEM((8, L), f32),
            pltpu.VMEM((4, 2 * NS, L), f32),
            pltpu.VMEM((2 * NS, L), f32),
            pltpu.VMEM((E, 4 * L), f32),
            pltpu.VMEM((E, L), f32),
            pltpu.VMEM((E, L), f32),
            pltpu.VMEM((E, L), bf16),
            pltpu.VMEM((8, E), f32),
            pltpu.VMEM((4, L, L), f32),
            pltpu.VMEM((4, A, L), f32),
            pltpu.VMEM((L, 2 * NS, L), f32),
            pltpu.VMEM((L, L), f32),
            pltpu.VMEM((2, 9, A, L), f32),
            pltpu.SemaphoreType.DMA((EXCHANGES,)),
            pltpu.SemaphoreType.DMA((EXCHANGES,)),
            pltpu.SemaphoreType.DMA((16,)),
        ],
        compiler_params=pltpu.CompilerParams(
            collective_id=0, has_side_effects=True, vmem_limit_bytes=60 * 1024 * 1024
        ),
    )(*given)
    new_features, charges, forces, virial = pl.pallas_call(
        hand_out,
        out_shape=(
            jax.ShapeDtypeStruct((A, L), bf16),
            jax.ShapeDtypeStruct((1, A), f32),
            jax.ShapeDtypeStruct((3, A), f32),
            jax.ShapeDtypeStruct((6, A), f32),
        ),
        in_specs=[vmem] * 2,
        out_specs=[hbm] * 4,
        scratch_shapes=[
            pltpu.VMEM((1, A), f32),
            pltpu.VMEM((3, A), f32),
            pltpu.VMEM((6, A), f32),
            pltpu.SemaphoreType.DMA((4,)),
        ],
    )(new_features, result)
    return new_features, charges.reshape(A), forces, virial


def solution(mesh):
    atoms = P(("row", "space"))
    columns = P(None, ("row", "space"))
    return jax.shard_map(
        shards,
        mesh=mesh,
        in_specs=(
            P(("row", "space"), None), columns, atoms, P("row", "space", None), atoms, atoms, columns,
        )
        + (P(),) * 9,
        out_specs=(P(("row", "space"), None), atoms, columns, columns),
        check_vma=False,
    )
```

time: 72 us -> 52.3 us (0.73)
  local copies, waits for them, and re-layouts: 11.5 us -> 0 us
  Pallas kernels: 58.5 us -> 50.8 us
    unnamed x34 -> x0, local copies, waits for them, and re-layouts: 11.5 us -> none
    pallas_call x1, Pallas kernels: 58.5 us -> 49.4 us  [shards(): pl.pallas_call(kernel, out_shape=(jax.ShapeDtypeStruct((A, L), bf16), jax...]
    pallas_call x0 -> x1, Pallas kernels: none -> 1.33 us  [shards(): pl.pallas_call(hand_out, out_shape=(jax.ShapeDtypeStruct((A, L), bf16), j...]
where the time goes in v2:
time: 52.3 us; the launch traced here: 52.1 us
  Pallas kernels  50.8 us (97%)
  between operations  1.29 us (2%)
    pallas_call x1, Pallas kernels, shards(): pl.pallas_call(kernel, out_shape=(jax.ShapeDtypeStruct((A, L), bf16), jax...  49.4 us
    pallas_call x1, Pallas kernels, shards(): pl.pallas_call(hand_out, out_shape=(jax.ShapeDtypeStruct((A, L), bf16), j...  1.33 us

profile of v2, /device:TPU:1, one launch (start us, length us, event | category | flops | bytes accessed | tf_op | source)
XLA Modules:
  0.0 52.1 jit_solution(3840754026429157287)
XLA Ops:
  1.3 49.4 %shard_map.183 = (bf16[16,128]{1,0:T(8,128)(2,1)}, f32[16,128]{1,0:T(8,128)}) custom-call(bf16[16,128]{1,0:T(8,128)(2,1)} %refs_0_.1, f32[3,16]{1,0:T(4,128)} %refs_1_.1, s32[1,16]{1,0:T(1,128)} %bitcast.7, s32[1,32,32]{2,1,0:T(8,128)} %refs_3_.1, s32[1,512]{1,0:T(1,128)} %bitcast.5, s32[1,512]{1,0:T(1,128)} %bitcast.6, f32[3,512]{1,0:T(4,128)} %refs_6_.1, ...), custom_call_target="tpu_custom_call" | custom-call | tf_op jit(solution)/shard_map/pallas_call | solution.py:395
  50.7 1.3 %shard_map.184 = (bf16[16,128]{1,0:T(8,128)(2,1)}, f32[1,16]{1,0:T(1,128)}, f32[3,16]{1,0:T(4,128)}, f32[6,16]{1,0:T(8,128)}) custom-call(bf16[16,128]{1,0:T(8,128)(2,1)} %get-tuple-element.10.nf, f32[16,128]{1,0:T(8,128)} %get-tuple-element.11.result), custom_call_target="tpu_custom_call" | custom-call | tf_op jit(solution)/shard_map/pallas_call | solution.py:432

commit v3 on v2

--- a/solution.py
+++ b/solution.py
@@ -27,7 +27,19 @@
 GROUPS = 8
 EXCHANGES = X_POS_P + GROUPS
 GROUP_ORDER = (0, 2, 6, 1, 4, 3, 7, 5)
-EARLY = 4
+EARLY = 2
+
+
+def hops(k):
+    return (0, 1, 2, 1)[k // 8] + (0, 1, 2, 1)[k // 2 % 4] + 0.3 * (k % 2)
+
+
+PEERS = sorted(range(1, NS), key=hops, reverse=True)
+PAIR_PEERS = sorted(
+    [(other, k) for other in (0, 1) for k in range(NS) if other or k],
+    key=lambda at: at[0] + hops(at[1]),
+    reverse=True,
+)
 
 f32 = jnp.float32
 bf16 = jnp.bfloat16
@@ -56,13 +68,13 @@
 
 def kernel(*refs):
     given = refs[:16]
-    nf_out, result_out = refs[16:18]
-    held = refs[18:34]
+    nf_out, q_out, f_out, v_out = refs[16:20]
+    held = refs[20:36]
     (
         lists, list_in, feat_in, own_in, packet, zpos, line, ppos, zvec, pair, vecs, psum,
         fil, base, slot, first, columns, coords, own_at, green, part, rows9,
-        send_sem, recv_sem, in_sem,
-    ) = refs[34:]
+        send_sem, recv_sem, in_sem, plane_ready, line_ready,
+    ) = refs[36:]
     (
         feat, pos, species, ghosts, recv, sender, evec, w_msg, w_rad1, w_rad2, w_up, w_out,
         hardness, width, chi_shift, field,
@@ -75,14 +87,27 @@
     def signal(device):
         pl.semaphore_signal(barrier, inc=1, device_id=device, device_id_type=MESH)
 
+    even = lax.rem(s, 2) == 0
+    mate = s + 1 - 2 * lax.rem(s, 2)
+
+    @pl.loop(0, NS // 2)
+    def _(k):
+        peer = 2 * lax.rem(s // 2 + k, NS // 2)
+
+        @pl.when(peer != s)
+        def _():
+            signal((z, peer))
+
     @pl.loop(1, NZ)
     def _(k):
-        signal((lax.rem(z + k, NZ), s))
-
-    @pl.loop(1, NS)
-    def _(k):
-        signal((z, lax.rem(s + k, NS)))
-        signal((twin, lax.rem(s + k, NS)))
+        signal((lax.rem(z + k, NZ), (s // 2) * 2 + 1))
+
+    @pl.when(even)
+    def _():
+        signal((z, mate))
+
+    def tell(semaphore):
+        pl.semaphore_signal(semaphore, inc=1, device_id=(z, mate), device_id_type=MESH)
 
     loads = [pltpu.make_async_copy(given[k], held[k], in_sem.at[k]) for k in range(16)]
     for load in loads:
@@ -99,26 +124,22 @@
         ).start()
 
     def send_z(which, src, dst, rows):
-        @pl.loop(1, NZ)
+        to = dst.at[pl.ds(z * rows, rows)]
+        send(which, src, to, (lax.rem(z + 8, NZ), s))
+
+        @pl.loop(1, 8)
         def _(k):
-            send(which, src, dst.at[pl.ds(z * rows, rows)], (lax.rem(z + k, NZ), s))
+            send(which, src, to, (lax.rem(z + 8 - k, NZ), s))
+            send(which, src, to, (lax.rem(z + 8 + k, NZ), s))
 
     def send_p(which, source, dst, rows):
         at = pl.multiple_of(s * rows, rows)
-
-        @pl.loop(1, NS)
-        def _(k):
-            peer = lax.rem(s + k, NS)
-            send(which, source(peer), dst.at[pl.ds(at, rows)], (z, peer))
+        for k in PEERS:
+            send(which, source(s ^ k), dst.at[pl.ds(at, rows)], (z, s ^ k))
 
     def send_two_planes(which, src, dst, at):
-        send(which, src, dst.at[pl.ds(at, 1)], (twin, s))
-
-        @pl.loop(1, NS)
-        def _(k):
-            peer = lax.rem(s + k, NS)
-            send(which, src, dst.at[pl.ds(at, 1)], (twin, peer))
-            send(which, src, dst.at[pl.ds(at, 1)], (z, peer))
+        for other, k in PAIR_PEERS:
+            send(which, src, dst.at[pl.ds(at, 1)], (twin if other else z, s ^ k))
 
     def await_rows(sem, dst, rows):
         some = dst.at[pl.ds(0, rows)]
@@ -183,6 +204,21 @@
     columns[4:5, :] = jnp.where(local, -1, ghost // NS).astype(f32)
     columns[5:6, :] = lax.rem(jnp.where(local, 0, ghost), NS).astype(f32)
     columns[6:8, :] = jnp.zeros((2, E), f32)
+
+    @pl.when(even)
+    def _():
+        pl.semaphore_wait(barrier, NS - 1)
+        tell(plane_ready)
+
+    @pl.when(jnp.logical_not(even))
+    def _():
+        pl.semaphore_wait(plane_ready, 1)
+
+    feat_at = pl.multiple_of(s * A, A)
+    for k in PEERS:
+        peer = s ^ k
+        send(X_LIST, lists.at[pl.ds(peer, 1)], list_in.at[pl.ds(s, 1)], (z, peer))
+        send(X_FEAT, feat, feat_in.at[pl.ds(feat_at, A)], (z, peer))
     turned = columns[...].T
     fil[:, 0:L] = filters[:, 0:L]
     for c in range(3):
@@ -193,25 +229,31 @@
     slot[...] = jnp.where(lane_f == turned[:, 5:6], 1.0, 0.0)
     receivers = jnp.where(iota((A, E), 0) == recv[...], 1.0, 0.0).astype(bf16)
 
-    pl.semaphore_wait(barrier, NZ + 2 * NS - 3)
-    send_p(X_LIST, lambda peer: lists.at[pl.ds(peer, 1)], list_in, 1)
-    send_p(X_FEAT, lambda peer: feat, feat_in, A)
+    @pl.when(even)
+    def _():
+        pl.semaphore_wait(line_ready, 1)
+
+    @pl.when(jnp.logical_not(even))
+    def _():
+        pl.semaphore_wait(barrier, 2 * NZ - 1)
+        tell(line_ready)
+
     send_z(X_POS_Z, packet, zpos, 8)
     list_in[pl.ds(s, 1), :] = lists[pl.ds(s, 1), :]
-    feat_in[pl.ds(pl.multiple_of(s * A, A), A), :] = feat[...]
+    feat_in[pl.ds(feat_at, A), :] = feat[...]
     zpos[pl.ds(pl.multiple_of(z * 8, 8), 8), :] = packet[...]
 
     await_rows(recv_sem.at[X_LIST], list_in, NS - 1)
     found = jnp.dot(first[...], list_in[...].astype(f32).astype(bf16), preferred_element_type=f32)
     found = (found * slot[...]).astype(bf16)
     found = jnp.dot(found, jnp.ones((L, L), bf16), preferred_element_type=f32)
-    await_rows(recv_sem.at[X_FEAT], feat_in, (NS - 1) * A)
     offset = base[...] - found
     picks = jnp.concatenate(
         [jnp.where(offset == float(-L * g), 1.0, 0.0).astype(bf16) for g in range(4)], axis=1
     )
-    picked = jnp.dot(picks, feat_in[...], preferred_element_type=f32).astype(bf16)
-    projected = jnp.dot(picked, w_msg[...], preferred_element_type=f32).astype(bf16).astype(f32)
+    await_rows(recv_sem.at[X_FEAT], feat_in, (NS - 1) * A)
+    table = jnp.dot(feat_in[...], w_msg[...], preferred_element_type=f32).astype(bf16)
+    projected = jnp.dot(picks, table, preferred_element_type=f32)
     lower, upper = projected[:, 0:L], projected[:, L:]
     message = jnp.concatenate(
         [(lower * fil[:, 0:L]).astype(bf16)]
@@ -241,14 +283,7 @@
         line[8 + h : 9 + h, :] = tile[4:5]
     own_group = s // 4
 
-    @pl.loop(1, NS)
-    def _(k):
-        peer = lax.rem(s + k, NS)
-        send(
-            X_POS_P + own_group, line.at[pl.ds(0, 8)],
-            ppos.at[pl.ds(pl.multiple_of(s * 8, 8), 8)], (z, peer),
-        )
-
+    send_p(X_POS_P + own_group, lambda peer: line.at[pl.ds(0, 8)], ppos, 8)
     ppos[pl.ds(pl.multiple_of(s * 8, 8), 8), :] = line[0:8, :]
     for c in range(4):
         spread_out = jnp.broadcast_to(line[pl.ds(chunk * 4 + c, 1), :], (L, L))
@@ -293,10 +328,18 @@
         @pl.loop(0, L, step=4)
         def _(i0):
             for i in range(4):
-                terms = green[i0 + i] * vector
-                part[pl.ds(i0 + i, 1), :] = jnp.sum(terms, axis=0, keepdims=True)
-
-        return jnp.sum(part[...].T, axis=0, keepdims=True)
+                terms = [
+                    green[i0 + i, 8 * g : 8 * g + 8, :] * vector[8 * g : 8 * g + 8]
+                    for g in range(GROUPS)
+                ]
+                while len(terms) > 1:
+                    terms = [a + b for a, b in zip(terms[::2], terms[1::2])]
+                part[pl.ds(pl.multiple_of((i0 + i) * 8, 8), 8), :] = terms[0]
+
+        rows = [part[pl.ds(k, L, stride=8), :] for k in range(8)]
+        while len(rows) > 1:
+            rows = [a + b for a, b in zip(rows[::2], rows[1::2])]
+        return jnp.sum(rows[0].T, axis=0, keepdims=True)
 
     def total(value):
         return jnp.sum(jnp.sum(value, axis=0, keepdims=True), axis=1, keepdims=True)
@@ -355,7 +398,10 @@
         result.append(0.5 * charge * moment[c])
     result.append(jnp.zeros((2, L), f32))
     result = jnp.concatenate(result, axis=0)
-    result_out[...] = pltpu.roll(result, lax.rem(L - off, L), axis=1)
+    result = pltpu.roll(result, lax.rem(L - off, L), axis=1)
+    q_out[...] = result[3:4, 0:A]
+    f_out[...] = result[0:3, 0:A]
+    v_out[...] = result[8:14, 0:A]
 
     for which, dst, rows in (
         (X_LIST, list_in, NS - 1),
@@ -370,14 +416,8 @@
         await_rows(send_sem.at[which], dst, rows)
 
 
-def hand_out(nf, result, nf_out, q_out, f_out, v_out, q, f, v, sem):
-    q[...] = result[3:4, 0:A]
-    f[...] = result[0:3, 0:A]
-    v[...] = result[8:14, 0:A]
-    copies = [
-        pltpu.make_async_copy(a, b, sem.at[k])
-        for k, (a, b) in enumerate(((nf, nf_out), (q, q_out), (f, f_out), (v, v_out)))
-    ]
+def hand_out(*refs):
+    copies = [pltpu.make_async_copy(refs[k], refs[4 + k], refs[8].at[k]) for k in range(4)]
     for copy in copies:
         copy.start()
     for copy in copies:
@@ -392,11 +432,17 @@
     hbm = pl.BlockSpec(memory_space=pltpu.HBM)
     held = [pltpu.VMEM(x.shape, x.dtype) for x in given[:12]]
     held += [pltpu.SMEM(x.shape, x.dtype) for x in given[12:]]
-    new_features, result = pl.pallas_call(
+    results = (
+        jax.ShapeDtypeStruct((A, L), bf16),
+        jax.ShapeDtypeStruct((1, A), f32),
+        jax.ShapeDtypeStruct((3, A), f32),
+        jax.ShapeDtypeStruct((6, A), f32),
+    )
+    made = pl.pallas_call(
         kernel,
-        out_shape=(jax.ShapeDtypeStruct((A, L), bf16), jax.ShapeDtypeStruct((16, L), f32)),
+        out_shape=results,
         in_specs=[hbm] * 16,
-        out_specs=[vmem] * 2,
+        out_specs=[vmem] * 4,
         scratch_shapes=held
         + [
             pltpu.VMEM((NS, L), jnp.int32),
@@ -419,11 +465,13 @@
             pltpu.VMEM((4, L, L), f32),
             pltpu.VMEM((4, A, L), f32),
             pltpu.VMEM((L, 2 * NS, L), f32),
-            pltpu.VMEM((L, L), f32),
+            pltpu.VMEM((8 * L, L), f32),
             pltpu.VMEM((2, 9, A, L), f32),
             pltpu.SemaphoreType.DMA((EXCHANGES,)),
             pltpu.SemaphoreType.DMA((EXCHANGES,)),
             pltpu.SemaphoreType.DMA((16,)),
+            pltpu.SemaphoreType.REGULAR,
+            pltpu.SemaphoreType.REGULAR,
         ],
         compiler_params=pltpu.CompilerParams(
             collective_id=0, has_side_effects=True, vmem_limit_bytes=60 * 1024 * 1024
@@ -431,21 +479,11 @@
     )(*given)
     new_features, charges, forces, virial = pl.pallas_call(
         hand_out,
-        out_shape=(
-            jax.ShapeDtypeStruct((A, L), bf16),
-            jax.ShapeDtypeStruct((1, A), f32),
-            jax.ShapeDtypeStruct((3, A), f32),
-            jax.ShapeDtypeStruct((6, A), f32),
-        ),
-        in_specs=[vmem] * 2,
+        out_shape=results,
+        in_specs=[hbm] * 4,
         out_specs=[hbm] * 4,
-        scratch_shapes=[
-            pltpu.VMEM((1, A), f32),
-            pltpu.VMEM((3, A), f32),
-            pltpu.VMEM((6, A), f32),
-            pltpu.SemaphoreType.DMA((4,)),
-        ],
-    )(new_features, result)
+        scratch_shapes=[pltpu.SemaphoreType.DMA((4,))],
+    )(*made)
     return new_features, charges.reshape(A), forces, virial
 
 

time: 52.3 us -> 50.2 us (0.960)
  Pallas kernels: 50.8 us -> 48.7 us
    pallas_call x2, Pallas kernels: 50.8 us -> 48.7 us  [the longest x1 47.3 us: shards(): pl.pallas_call(kernel, out_shape=results, in_specs=[hbm] * 16, out_specs=...]
where the time goes in v3:
time: 50.2 us; the launch traced here: 50 us
  Pallas kernels  48.7 us (97%)
  between operations  1.29 us (3%)
    pallas_call x1, Pallas kernels, shards(): pl.pallas_call(kernel, out_shape=results, in_specs=[hbm] * 16, out_specs=...  47.3 us
    pallas_call x1, Pallas kernels, shards(): pl.pallas_call(hand_out, out_shape=results, in_specs=[hbm] * 4, out_specs...  1.42 us

profile of v3, /device:TPU:1, one launch (start us, length us, event | category | flops | bytes accessed | tf_op | source)
XLA Modules:
  0.0 50.0 jit_solution(1368985718744161261)
XLA Ops:
  1.3 47.3 %shard_map.183 = (bf16[16,128]{1,0:T(8,128)(2,1)}, f32[1,16]{1,0:T(1,128)}, f32[3,16]{1,0:T(4,128)}, f32[6,16]{1,0:T(8,128)}) custom-call(bf16[16,128]{1,0:T(8,128)(2,1)} %refs_0_.1, f32[3,16]{1,0:T(4,128)} %refs_1_.1, s32[1,16]{1,0:T(1,128)} %bitcast.7, s32[1,32,32]{2,1,0:T(8,128)} %refs_3_.1, s32[1,512]{1,0:T(1,128)} %bitcast.5, s32[1,512]{1,0:T(1,128)} %bitcast.6, ...), custom_call_target="tpu_custom_call" | custom-call | tf_op jit(solution)/shard_map/pallas_call | solution.py:441
  48.6 1.4 %shard_map.184 = (bf16[16,128]{1,0:T(8,128)(2,1)}, f32[1,16]{1,0:T(1,128)}, f32[3,16]{1,0:T(4,128)}, f32[6,16]{1,0:T(8,128)}) custom-call(bf16[16,128]{1,0:T(8,128)(2,1)} %get-tuple-element.12.refs_0_, f32[1,16]{1,0:T(1,128)} %get-tuple-element.13.refs_1_, f32[3,16]{1,0:T(4,128)} %get-tuple-element.14.refs_2_, f32[6,16]{1,0:T(8,128)} %get-tuple-element.15.refs_3_), custom_call_target="tpu_custom_call" | custom-call | tf_op jit(solution)/shard_map/pallas_call | solution.py:480

commit v4 on v3

--- a/solution.py
+++ b/solution.py
@@ -18,6 +18,7 @@
 CUTOFF = 6.0
 MESSAGE_SCALE = 0.125
 TWO_OVER_ROOT_PI = 2.0 / math.sqrt(math.pi)
+LOG2E = math.log2(math.e)
 INVERSE_ROOT_PI = 1.0 / math.sqrt(math.pi)
 
 ERF_P = 0.55
@@ -27,7 +28,7 @@
 GROUPS = 8
 EXCHANGES = X_POS_P + GROUPS
 GROUP_ORDER = (0, 2, 6, 1, 4, 3, 7, 5)
-EARLY = 2
+EARLY = 1
 
 
 def hops(k):
@@ -58,12 +59,12 @@
     inverse = lax.rsqrt(r2)
     scale = lax.rsqrt(spread)
     x = r2 * inverse * scale
-    bell = jnp.exp(-(x * x))
-    t = reciprocal(1.0 + ERF_P * x)
+    bell = jnp.exp2(-(x * x))
+    t = reciprocal(1.0 + (ERF_P / math.sqrt(LOG2E)) * x)
     poly = ERF_C[5]
     for c in ERF_C[4::-1]:
         poly = poly * t + c
-    return (1.0 - bell * (poly * t)) * inverse, TWO_OVER_ROOT_PI * scale * bell, inverse
+    return (1.0 - bell * (poly * t)) * inverse, (TWO_OVER_ROOT_PI / math.sqrt(LOG2E)) * scale * bell, inverse
 
 
 def kernel(*refs):
@@ -170,11 +171,16 @@
         return out
 
     sigma = jnp.where(mine, lookup(width), 1.0)
-    spread = jnp.where(mine, 2.0 * sigma * sigma, 0.0)
+    spread = jnp.where(mine, (2.0 / LOG2E) * sigma * sigma, 0.0)
     packet[0:3, :] = own[0:3]
     packet[3:4, :] = spread
     packet[4:5, :] = jnp.where(mine, lookup(hardness) + INVERSE_ROOT_PI / sigma, 0.0)
     packet[5:8, :] = jnp.zeros((3, L), f32)
+    back = pltpu.roll(packet[...], lax.rem(L - off, L), axis=1)
+    folded = back[0:1]
+    for c in range(1, 5):
+        folded = folded + pltpu.roll(back[c : c + 1], A * c, axis=1)
+    line[12:13, :] = folded
     for c in range(4):
         column = jnp.sum(jnp.where(diagonal, packet[c : c + 1, :], 0.0), axis=1, keepdims=True)
         own_at[c] = jnp.broadcast_to(column, (A, L))
@@ -238,10 +244,10 @@
         pl.semaphore_wait(barrier, 2 * NZ - 1)
         tell(line_ready)
 
-    send_z(X_POS_Z, packet, zpos, 8)
+    send_z(X_POS_Z, line.at[pl.ds(12, 1)], zpos, 1)
     list_in[pl.ds(s, 1), :] = lists[pl.ds(s, 1), :]
     feat_in[pl.ds(feat_at, A), :] = feat[...]
-    zpos[pl.ds(pl.multiple_of(z * 8, 8), 8), :] = packet[...]
+    zpos[pl.ds(z, 1), :] = line[12:13, :]
 
     await_rows(recv_sem.at[X_LIST], list_in, NS - 1)
     found = jnp.dot(first[...], list_in[...].astype(f32).astype(bf16), preferred_element_type=f32)
@@ -274,13 +280,18 @@
     zvec[pl.ds(z, 1), :] = rhs
     send_z(X_B_Z, pair.at[pl.ds(2, 1)], zvec, 1)
 
-    await_rows(recv_sem.at[X_POS_Z], zpos, (NZ - 1) * 8)
+    await_rows(recv_sem.at[X_POS_Z], zpos, NZ - 1)
+    tall, wide = iota((8, L), 0), iota((8, L), 1) // A
+    masks = [(tall == r) & (wide == r) for r in range(8)]
     for h in range(2):
-        tile = zpos[h * 64 : h * 64 + 8, :]
-        for t in range(1, 8):
-            tile = tile + zpos[h * 64 + 8 * t : h * 64 + 8 * t + 8, :]
-        line[h * 4 : h * 4 + 4, :] = tile[0:4]
-        line[8 + h : 9 + h, :] = tile[4:5]
+        tile = zpos[8 * h : 8 * h + 8, :]
+        shifted = [tile] + [pltpu.roll(tile, A * d, axis=1) for d in range(1, 8)]
+        for c in range(5):
+            terms = [jnp.where(masks[r], shifted[(r - c) % 8], 0.0) for r in range(8)]
+            while len(terms) > 1:
+                terms = [a + b for a, b in zip(terms[::2], terms[1::2])]
+            at_line = h * 4 + c if c < 4 else 8 + h
+            line[at_line : at_line + 1, :] = jnp.sum(terms[0], axis=0, keepdims=True)
     own_group = s // 4
 
     send_p(X_POS_P + own_group, lambda peer: line.at[pl.ds(0, 8)], ppos, 8)
@@ -302,7 +313,9 @@
             for i in range(8):
                 at = [coords[c, pl.ds(i0 + i, 1), :] for c in range(4)]
                 dx, dy, dz = (at[c] - xs[c] for c in range(3))
-                r2 = jnp.maximum(dx * dx + dy * dy + dz * dz, 1.0)
+                r2 = dx * dx + dy * dy + dz * dz
+                if turn == 0:
+                    r2 = jnp.maximum(r2, 1.0)
                 value = smeared(r2, at[3] + xs[3])[0]
                 if turn == 0:
                     itself = (iota((8, L), 0) == own_at_row) & (iota((8, L), 1) == i0 + i)
@@ -406,7 +419,7 @@
     for which, dst, rows in (
         (X_LIST, list_in, NS - 1),
         (X_FEAT, feat_in, (NS - 1) * A),
-        (X_POS_Z, zpos, (NZ - 1) * 8),
+        (X_POS_Z, zpos, NZ - 1),
         (X_POS_P + own_group, ppos, (NS - 1) * 8),
         (X_B_Z, zvec, NZ - 1),
         (X_B_P, vecs.at[0], (NS - 1) * 2),
@@ -450,7 +463,7 @@
             pltpu.VMEM((NS * A, L), bf16),
             pltpu.VMEM((8, L), f32),
             pltpu.VMEM((8, L), f32),
-            pltpu.VMEM((NZ * 8, L), f32),
+            pltpu.VMEM((NZ, L), f32),
             pltpu.VMEM((16, L), f32),
             pltpu.VMEM((NS * 8, L), f32),
             pltpu.VMEM((NZ, L), f32),

time: 50.2 us -> 49.7 us (0.990)
    pallas_call x1, Pallas kernels: 47.3 us -> 46.8 us  [shards(): pl.pallas_call(kernel, out_shape=results, in_specs=[hbm] * 16, out_specs=...]
where the time goes in v4:
time: 49.7 us; the launch traced here: 49.5 us
  Pallas kernels  48.2 us (97%)
  between operations  1.29 us (3%)
    pallas_call x1, Pallas kernels, shards(): pl.pallas_call(kernel, out_shape=results, in_specs=[hbm] * 16, out_specs=...  46.8 us
    pallas_call x1, Pallas kernels, shards(): pl.pallas_call(hand_out, out_shape=results, in_specs=[hbm] * 4, out_specs...  1.42 us

profile of v4, /device:TPU:1, one launch (start us, length us, event | category | flops | bytes accessed | tf_op | source)
XLA Modules:
  0.0 49.5 jit_solution(6912553854146623826)
XLA Ops:
  1.3 46.8 %shard_map.183 = (bf16[16,128]{1,0:T(8,128)(2,1)}, f32[1,16]{1,0:T(1,128)}, f32[3,16]{1,0:T(4,128)}, f32[6,16]{1,0:T(8,128)}) custom-call(bf16[16,128]{1,0:T(8,128)(2,1)} %refs_0_.1, f32[3,16]{1,0:T(4,128)} %refs_1_.1, s32[1,16]{1,0:T(1,128)} %bitcast.7, s32[1,32,32]{2,1,0:T(8,128)} %refs_3_.1, s32[1,512]{1,0:T(1,128)} %bitcast.5, s32[1,512]{1,0:T(1,128)} %bitcast.6, ...), custom_call_target="tpu_custom_call" | custom-call | tf_op jit(solution)/shard_map/pallas_call | solution.py:454
  48.1 1.4 %shard_map.184 = (bf16[16,128]{1,0:T(8,128)(2,1)}, f32[1,16]{1,0:T(1,128)}, f32[3,16]{1,0:T(4,128)}, f32[6,16]{1,0:T(8,128)}) custom-call(bf16[16,128]{1,0:T(8,128)(2,1)} %get-tuple-element.12.refs_0_, f32[1,16]{1,0:T(1,128)} %get-tuple-element.13.refs_1_, f32[3,16]{1,0:T(4,128)} %get-tuple-element.14.refs_2_, f32[6,16]{1,0:T(8,128)} %get-tuple-element.15.refs_3_), custom_call_target="tpu_custom_call" | custom-call | tf_op jit(solution)/shard_map/pallas_call | solution.py:493
